TPU v7x, 32 devices: a whole 2x2x4 slice. The times are simulated.
32 devices in a mesh: fsdp: 16 (over z, y, core), dp: 2 (over x).
Axes of the slice: x: 2, y: 2, z: 4, core: 2. Of those that a mesh axis runs over, the one named last changes fastest.
Arguments:
- tokens: bfloat16 [32, 512, 768], P(('fsdp', 'dp')), may hold values from -6 to 6
- cotangent: bfloat16 [32, 512, 768], P(('fsdp', 'dp')), may hold values from -6 to 6
- lengths: int32 [32], P(('fsdp', 'dp')), may hold values from 64 to 512, as said below
- matrices: float32 [48, 384, 384], P(None, 'fsdp')
- first_moment: float32 [48, 384, 384], P(None, 'fsdp')
- second_moment: float32 [48, 384, 384], P(None, 'fsdp'), as said below
- left_stat: float32 [48, 384, 384], P(None, 'fsdp'), as said below
- right_stat: float32 [48, 384, 384], P(None, 'fsdp'), as said below
- left_basis: float32 [48, 384, 384], P(None, 'fsdp'), as said below
- right_basis: float32 [48, 384, 384], P(None, 'fsdp'), as said below
- vectors: float32 [9216], P('fsdp')
- vector_first: float32 [9216], P('fsdp')
- vector_second: float32 [9216], P('fsdp'), as said below
Outputs:
- block_out: bfloat16 [32, 512, 768], P(('fsdp', 'dp'))
- input_grad: float32 [32, 512, 768], P(('fsdp', 'dp'))
- new_matrices: float32 [48, 384, 384], P(None, 'fsdp')
- matrices_low: bfloat16 [48, 384, 384], P(None, 'fsdp')
- new_first: float32 [48, 384, 384], P(None, 'fsdp')
- new_second: float32 [48, 384, 384], P(None, 'fsdp')
- new_left_stat: float32 [48, 384, 384], P(None, 'fsdp')
- new_right_stat: float32 [48, 384, 384], P(None, 'fsdp')
- new_left_basis: float32 [48, 384, 384], P(None, 'fsdp')
- new_right_basis: float32 [48, 384, 384], P(None, 'fsdp')
- vector_first_new: float32 [9216], P('fsdp')
- vector_second_new: float32 [9216], P('fsdp')
- vector_new: float32 [9216], P('fsdp')
Inputs may be any that keep to these rules, and one draw needn't show every extreme that they name: `lengths`: positions from a sequence's length to 512 are padding; in every draw some sequence is full. `left_basis`: each block is orthogonal. `right_basis`: each block is orthogonal. `left_stat`: each block is symmetric and diagonally dominant with a positive diagonal. `right_stat`: each block is symmetric and diagonally dominant with a positive diagonal. `second_moment`: Positive. `vector_second`: Positive.
All inputs are finite; a program needn't handle non-finite values.
Results may differ from a plain program's by a relative error of at most 0.014.
The roundings to bfloat16 on the way count: a program that leaves them out, or rounds other values in their place, can miss the bound.
Values may be sent and summed in bfloat16 or wider, within the bound.
A program may use at most 256 MiB of HBM per device.

v0:
```python
import jax
import jax.numpy as jnp
from jax import lax
from jax.sharding import PartitionSpec as P

HEADS = 12
HEAD_DIM = 64
FF = 3072
ADAM_STEP = 10


PRECISE = lax.Precision.HIGHEST
FIRST_DECAY = 0.9
SECOND_DECAY = 0.999
STAT_DECAY = 0.95
ADAM_EPSILON = 1e-08
NORM_EPSILON = 1e-05
MATRIX_RATE = 0.03
VECTOR_RATE = 0.2
WEIGHT_DECAY = 0.01


def as_sent(x):

    def short(part):
        return part.astype(jnp.bfloat16) if part.dtype == jnp.float32 else part

    return jax.tree.map(short, x)


def assemble(blocks, row_count, column_count):
    block_side = blocks.shape[-1]
    shaped = blocks.reshape(row_count, column_count, block_side, block_side)
    return shaped.transpose(0, 2, 1, 3).reshape(row_count * block_side, column_count * block_side)


def split_blocks(matrix, row_count, column_count, block_side):
    shaped = matrix.reshape(row_count, block_side, column_count, block_side)
    return shaped.transpose(0, 2, 1, 3).reshape(row_count * column_count, block_side, block_side)


def layer_norm(values, gain_row, shift_row):
    center = jnp.mean(values, axis=-1, keepdims=True)
    centered = values - center
    spread = jnp.mean(centered * centered, axis=-1, keepdims=True)
    return centered * lax.rsqrt(spread + NORM_EPSILON) * gain_row + shift_row


def exact_gelu(hidden):
    return jax.nn.gelu(hidden, approximate=False)


def masked_scores(heads_query, heads_key, length):
    slots = heads_query.shape[0]
    scores = jnp.einsum(
        "qhd,khd->hqk", heads_query, heads_key, preferred_element_type=jnp.float32
    ) * HEAD_DIM ** (-0.5)
    visible = lax.iota(jnp.int32, slots) < length
    return jnp.where(visible[None, None, :], scores, -1e30)


def attend(pieces):
    query_rows, key_rows, value_rows, length = pieces
    slots = query_rows.shape[0]
    heads_query = query_rows.reshape(slots, HEADS, HEAD_DIM)
    heads_key = key_rows.reshape(slots, HEADS, HEAD_DIM)
    heads_value = value_rows.reshape(slots, HEADS, HEAD_DIM)
    scores = masked_scores(heads_query, heads_key, length)
    row_max = jnp.max(scores, axis=-1, keepdims=True)
    shifted = jnp.exp(scores - row_max)
    row_total = jnp.sum(shifted, axis=-1, keepdims=True)
    attention_weights = (shifted / row_total).astype(jnp.bfloat16)
    context = jnp.einsum(
        "hqk,khd->qhd", attention_weights, heads_value, preferred_element_type=jnp.float32
    )
    return (
        context.reshape(slots, -1).astype(jnp.bfloat16),
        row_max[..., 0] + jnp.log(row_total[..., 0]),
    )


def attend_back(pieces):
    query_rows, key_rows, value_rows, logsum, grad_context, length = pieces
    slots = query_rows.shape[0]
    heads_query = query_rows.reshape(slots, HEADS, HEAD_DIM)
    heads_key = key_rows.reshape(slots, HEADS, HEAD_DIM)
    heads_value = value_rows.reshape(slots, HEADS, HEAD_DIM)
    heads_grad = grad_context.reshape(slots, HEADS, HEAD_DIM)
    scores = masked_scores(heads_query, heads_key, length)
    attention_weights = jnp.exp(scores - logsum[..., None])
    weights_low = attention_weights.astype(jnp.bfloat16)
    grad_values = jnp.einsum(
        "hqk,qhd->khd", weights_low, heads_grad, preferred_element_type=jnp.float32
    )
    grad_weights = jnp.einsum(
        "qhd,khd->hqk", heads_grad, heads_value, preferred_element_type=jnp.float32
    )
    grad_scores = attention_weights * (
        grad_weights - jnp.sum(grad_weights * attention_weights, axis=-1, keepdims=True)
    )
    scores_low = grad_scores.astype(jnp.bfloat16)
    grad_query = jnp.einsum(
        "hqk,khd->qhd", scores_low, heads_key, preferred_element_type=jnp.float32
    ) * HEAD_DIM ** (-0.5)
    grad_keys = jnp.einsum(
        "hqk,qhd->khd", scores_low, heads_query, preferred_element_type=jnp.float32
    ) * HEAD_DIM ** (-0.5)
    return (
        grad_query.reshape(slots, -1).astype(jnp.bfloat16),
        grad_keys.reshape(slots, -1).astype(jnp.bfloat16),
        grad_values.reshape(slots, -1).astype(jnp.bfloat16),
    )


def orthonormal(matrix):
    block_side = matrix.shape[-1]
    gram_matrix = jnp.einsum("kai,kaj->kij", matrix, matrix, precision=PRECISE)
    vacant = jnp.all(matrix == 0.0, axis=(1, 2))
    gram_matrix = jnp.where(
        vacant[:, None, None], jnp.eye(block_side, dtype=jnp.float32), gram_matrix
    )
    lower_factor = jnp.linalg.cholesky(gram_matrix)

    def solve_one(factor, target):
        return jax.scipy.linalg.solve_triangular(factor, target, lower=True)

    solved = jax.vmap(solve_one)(lower_factor, jnp.swapaxes(matrix, 1, 2))
    return jnp.swapaxes(solved, 1, 2)


def soap_blocks(states):
    gradient, first_moment, second_moment, left_stat, right_stat, left_basis, right_basis = [
        states[:, member] for member in range(7)
    ]
    rotated = jnp.einsum("kai,kab->kib", left_basis, gradient, precision=PRECISE)
    rotated = jnp.einsum("kib,kbj->kij", rotated, right_basis, precision=PRECISE)
    first_new = FIRST_DECAY * first_moment + (1.0 - FIRST_DECAY) * rotated
    second_new = SECOND_DECAY * second_moment + (1.0 - SECOND_DECAY) * rotated * rotated
    direction = (
        first_new
        / (1.0 - FIRST_DECAY**ADAM_STEP)
        / (jnp.sqrt(second_new / (1.0 - SECOND_DECAY**ADAM_STEP)) + ADAM_EPSILON)
    )
    turned = jnp.einsum("kia,kab->kib", left_basis, direction, precision=PRECISE)
    update = jnp.einsum("kib,kjb->kij", turned, right_basis, precision=PRECISE)
    left_new = STAT_DECAY * left_stat + (1.0 - STAT_DECAY) * jnp.einsum(
        "kia,kja->kij", gradient, gradient, precision=PRECISE
    )
    right_new = STAT_DECAY * right_stat + (1.0 - STAT_DECAY) * jnp.einsum(
        "kai,kaj->kij", gradient, gradient, precision=PRECISE
    )
    left_turn = orthonormal(jnp.einsum("kia,kaj->kij", left_new, left_basis, precision=PRECISE))
    right_turn = orthonormal(jnp.einsum("kia,kaj->kij", right_new, right_basis, precision=PRECISE))
    return jnp.stack(
        [update, first_new, second_new, left_new, right_new, left_turn, right_turn], axis=1
    )


def shards(
    tokens,
    cotangent,
    lengths,
    matrices,
    first_moment,
    second_moment,
    left_stat,
    right_stat,
    left_basis,
    right_basis,
    vectors,
    vector_first,
    vector_second,
):
    shard_count = lax.axis_size("fsdp")
    sequences, slots, model_width = tokens.shape
    block_side = matrices.shape[-1]
    block_total = matrices.shape[0]
    row_blocks = model_width // block_side
    column_blocks = FF // block_side
    square = row_blocks * row_blocks
    attn_end = 4 * square
    down_start = row_blocks * column_blocks
    unit_ratio = FF // model_width
    rows_total = sequences * slots

    def shaped(array):
        return array.reshape(sequences, slots, array.shape[-1])

    low_matrices = matrices.astype(jnp.bfloat16)
    gathered_attn, gathered_vec = (
        lax.all_gather(low_matrices[:attn_end], "fsdp", axis=1, tiled=True),
        lax.all_gather(vectors.astype(jnp.bfloat16), "fsdp", axis=0, tiled=True),
    )
    vector_rows = gathered_vec.astype(jnp.float32).reshape(-1, model_width)
    weight_qkv = jnp.concatenate(
        [
            assemble(
                gathered_attn[part_index * square : (part_index + 1) * square],
                row_blocks,
                row_blocks,
            )
            for part_index in range(3)
        ],
        axis=1,
    )
    weight_out = assemble(gathered_attn[3 * square :], row_blocks, row_blocks)
    inputs = tokens.reshape(rows_total, model_width)
    joined = jnp.dot(inputs, weight_qkv, preferred_element_type=jnp.float32)
    query_rows = (joined[:, :model_width] + vector_rows[0]).astype(jnp.bfloat16)
    key_rows = joined[:, model_width : 2 * model_width].astype(jnp.bfloat16)
    value_rows = (joined[:, 2 * model_width :] + vector_rows[1]).astype(jnp.bfloat16)
    context, logsum = lax.map(
        attend, (shaped(query_rows), shaped(key_rows), shaped(value_rows), lengths)
    )
    context = context.reshape(rows_total, model_width)
    attended = jnp.dot(context, weight_out, preferred_element_type=jnp.float32) + vector_rows[2]
    normed, pull_one = jax.vjp(
        layer_norm, inputs.astype(jnp.float32) + attended, vector_rows[3], vector_rows[4]
    )
    normed_low = normed.astype(jnp.bfloat16)
    gathered_ffn = lax.all_gather(low_matrices[attn_end:], "fsdp", axis=1, tiled=True)
    weight_up = assemble(gathered_ffn[:down_start], row_blocks, column_blocks)
    weight_down = assemble(gathered_ffn[down_start:], column_blocks, row_blocks)
    hidden = jnp.dot(normed_low, weight_up, preferred_element_type=jnp.float32) + vector_rows[
        5 : 5 + unit_ratio
    ].reshape(FF)
    active, pull_gelu = jax.vjp(exact_gelu, hidden)
    active_low = active.astype(jnp.bfloat16)
    result = (
        jnp.dot(active_low, weight_down, preferred_element_type=jnp.float32)
        + vector_rows[5 + unit_ratio]
    )
    output, pull_two = jax.vjp(
        layer_norm, normed + result, vector_rows[6 + unit_ratio], vector_rows[7 + unit_ratio]
    )
    block_out = output.reshape(sequences, slots, model_width).astype(jnp.bfloat16)
    visible = (lax.iota(jnp.int32, slots)[None, :] < lengths[:, None]).astype(jnp.float32)
    grad_output = (cotangent.astype(jnp.float32) * visible[:, :, None]).reshape(
        rows_total, model_width
    )
    grad_second, grad_gain_two, grad_shift_two = pull_two(grad_output)
    second_low = grad_second.astype(jnp.bfloat16)
    again_ffn = lax.all_gather(low_matrices[attn_end:], "fsdp", axis=1, tiled=True)
    back_up = assemble(again_ffn[:down_start], row_blocks, column_blocks)
    back_down = assemble(again_ffn[down_start:], column_blocks, row_blocks)
    grad_down = jnp.einsum("tf,td->fd", active_low, second_low, preferred_element_type=jnp.float32)
    grad_active = jnp.einsum("td,fd->tf", second_low, back_down, preferred_element_type=jnp.float32)
    (grad_hidden,) = pull_gelu(grad_active)
    hidden_low = grad_hidden.astype(jnp.bfloat16)
    grad_up = jnp.einsum("td,tf->df", normed_low, hidden_low, preferred_element_type=jnp.float32)
    grad_normed = grad_second + jnp.einsum(
        "tf,df->td", hidden_low, back_up, preferred_element_type=jnp.float32
    )
    ffn_blocks = jnp.concatenate(
        [
            split_blocks(grad_up, row_blocks, column_blocks, block_side),
            split_blocks(grad_down, column_blocks, row_blocks, block_side),
        ],
        axis=0,
    )
    grad_mixed, grad_gain_one, grad_shift_one = pull_one(grad_normed)
    mixed_low = grad_mixed.astype(jnp.bfloat16)
    again_attn = lax.all_gather(low_matrices[:attn_end], "fsdp", axis=1, tiled=True)
    back_qkv = jnp.concatenate(
        [
            assemble(
                again_attn[part_index * square : (part_index + 1) * square], row_blocks, row_blocks
            )
            for part_index in range(3)
        ],
        axis=1,
    )
    back_out = assemble(again_attn[3 * square :], row_blocks, row_blocks)
    grad_out_weight = jnp.einsum(
        "td,te->de", context, mixed_low, preferred_element_type=jnp.float32
    )
    grad_context = jnp.einsum(
        "te,de->td", mixed_low, back_out, preferred_element_type=jnp.float32
    ).astype(jnp.bfloat16)
    grad_query, grad_keys, grad_values = lax.map(
        attend_back,
        (
            shaped(query_rows),
            shaped(key_rows),
            shaped(value_rows),
            logsum,
            shaped(grad_context),
            lengths,
        ),
    )
    grad_joined = jnp.concatenate(
        [
            grad_query.reshape(rows_total, model_width),
            grad_keys.reshape(rows_total, model_width),
            grad_values.reshape(rows_total, model_width),
        ],
        axis=1,
    )
    grad_qkv = jnp.einsum("td,te->de", inputs, grad_joined, preferred_element_type=jnp.float32)
    input_grad = grad_mixed + jnp.einsum(
        "te,de->td", grad_joined, back_qkv, preferred_element_type=jnp.float32
    )
    attn_blocks = jnp.concatenate(
        [
            split_blocks(
                grad_qkv[:, part_index * model_width : (part_index + 1) * model_width],
                row_blocks,
                row_blocks,
                block_side,
            )
            for part_index in range(3)
        ]
        + [split_blocks(grad_out_weight, row_blocks, row_blocks, block_side)],
        axis=0,
    )
    vector_grad = jnp.concatenate(
        [
            jnp.sum(grad_joined[:, :model_width], axis=0, dtype=jnp.float32)[None],
            jnp.sum(grad_joined[:, 2 * model_width :], axis=0, dtype=jnp.float32)[None],
            jnp.sum(grad_mixed, axis=0)[None],
            grad_gain_one[None],
            grad_shift_one[None],
            jnp.sum(grad_hidden, axis=0).reshape(unit_ratio, model_width),
            jnp.sum(grad_second, axis=0)[None],
            grad_gain_two[None],
            grad_shift_two[None],
        ],
        axis=0,
    ).reshape(-1)
    grad_share, vector_share = (
        lax.psum_scatter(
            jnp.concatenate([attn_blocks, ffn_blocks], axis=0),
            "fsdp",
            scatter_dimension=1,
            tiled=True,
        ),
        lax.psum_scatter(vector_grad, "fsdp", scatter_dimension=0, tiled=True),
    )
    grad_share, vector_share = (
        lax.psum(grad_share.astype(jnp.bfloat16), "dp").astype(jnp.float32),
        lax.psum(vector_share.astype(jnp.bfloat16), "dp").astype(jnp.float32),
    )
    capacity = -(-block_total // shard_count)
    block_list = lax.iota(jnp.int32, block_total)
    owner_of = block_list % shard_count
    position = block_list // shard_count
    slot_of = owner_of * capacity + position
    selector = (lax.iota(jnp.int32, shard_count * capacity)[:, None] == slot_of[None, :]).astype(
        jnp.float32
    )
    states = jnp.stack(
        [grad_share, first_moment, second_moment, left_stat, right_stat, left_basis, right_basis],
        axis=1,
    )
    share_rows = states.shape[2]
    outgoing = jnp.einsum("sb,bc->sc", selector, states.reshape(block_total, -1), precision=PRECISE)
    outgoing = outgoing.reshape(shard_count, capacity, 7, share_rows, block_side)
    results = soap_blocks(
        lax.all_to_all(
            outgoing.astype(jnp.bfloat16), "fsdp", split_axis=0, concat_axis=3, tiled=True
        ).astype(outgoing.dtype)[0]
    )
    returned = lax.all_to_all(
        as_sent(results[None]), "fsdp", split_axis=3, concat_axis=0, tiled=True
    )
    local = jnp.einsum(
        "sb,sc->bc", selector, returned.reshape(shard_count * capacity, -1), precision=PRECISE
    )
    local = local.reshape(block_total, 7, share_rows, block_side)
    new_matrices = matrices - MATRIX_RATE * (local[:, 0] + WEIGHT_DECAY * matrices)
    vfirst_new = FIRST_DECAY * vector_first + (1.0 - FIRST_DECAY) * vector_share
    vsecond_new = SECOND_DECAY * vector_second + (1.0 - SECOND_DECAY) * vector_share * vector_share
    vector_new = vectors - VECTOR_RATE * (vfirst_new / (1.0 - FIRST_DECAY**ADAM_STEP)) / (
        jnp.sqrt(vsecond_new / (1.0 - SECOND_DECAY**ADAM_STEP)) + ADAM_EPSILON
    )
    return (
        block_out,
        input_grad.reshape(sequences, slots, model_width),
        new_matrices,
        new_matrices.astype(jnp.bfloat16),
        local[:, 1],
        local[:, 2],
        local[:, 3],
        local[:, 4],
        local[:, 5],
        local[:, 6],
        vfirst_new,
        vsecond_new,
        vector_new,
    )


def solution(mesh):
    return jax.shard_map(
        shards,
        mesh=mesh,
        in_specs=(
            P(("fsdp", "dp"), None, None),
            P(("fsdp", "dp"), None, None),
            P(("fsdp", "dp")),
            P(None, "fsdp", None),
            P(None, "fsdp", None),
            P(None, "fsdp", None),
            P(None, "fsdp", None),
            P(None, "fsdp", None),
            P(None, "fsdp", None),
            P(None, "fsdp", None),
            P("fsdp"),
            P("fsdp"),
            P("fsdp"),
        ),
        out_specs=(
            P(("fsdp", "dp"), None, None),
            P(("fsdp", "dp"), None, None),
            P(None, "fsdp", None),
            P(None, "fsdp", None),
            P(None, "fsdp", None),
            P(None, "fsdp", None),
            P(None, "fsdp", None),
            P(None, "fsdp", None),
            P(None, "fsdp", None),
            P(None, "fsdp", None),
            P("fsdp"),
            P("fsdp"),
            P("fsdp"),
        ),
        check_vma=False,
    )
```

profile of v0, /device:TPU:12, one launch (start us, length us, event | category | flops | bytes accessed | tf_op | source)
XLA Modules:
  0.0 1759.6 jit_solution(5990357960536735002)
XLA Ops:
  12.2 50.1 %all-reduce.1 = bf16[9216]{0:T(1024)(128)(2,1)S(1)} all-reduce(bf16[9216]{0:T(1024)(128)(2,1)S(1)} %dynamic-update-slice.13), channel_id=1, replica_groups=mesh['fsdp'=16,'dp'=2] {'fsdp'}, use_global_device_ids=true, to_apply=%add.1 | all-reduce | flops 9216 | bytes 36864
  90.3 56.8 %all-gather.5.cloned.1.call-done = bf16[32,384,384]{2,1,0:T(8,128)(2,1)} async-done(((bf16[32,24,384]{2,1,0:T(8,128)(2,1)}), bf16[32,384,384]{2,1,0:T(8,128)(2,1)}) %all-gather.5.cloned.1.call-update) | async-done | bytes 9437200 | tf_op jit(solution)/shard_map/all_gather | solution.py:221
  147.1 7.2 fusion.150
  160.4 7.0 copy.318
  171.7 18.1 %multiply_convert_fusion.1 = (bf16[512,3072]{1,0:T(8,128)(2,1)S(1)}, f32[512,3072]{1,0:T(8,128)S(1)}, f32[512,3072]{1,0:T(8,128)}) fusion(f32[3072]{0:T(1024)S(1)} %slice.253, bf16[768,3072]{1,0:T(8,128)(2,1)S(1)} %bitcast.447, f32[512,768]{1,0:T(8,128)S(1)} %copy-done.20, f32[768]{0:T(1024)S(1)} %get-tuple-element.223, f32[768]{0:T(1024)S(1)} %get-tuple-element.222, ...), kind=kOutput, calls=%fused_computation.21 | convolution fusion | flops 2521694208 | bytes 22042624 | tf_op jit(solution)/shard_map/dot_general | solution.py:224
  196.7 8.1 fusion.159
  213.4 7.5 convert_reduce_fusion
  220.9 9.3 multiply_reduce_fusion
  300.9 12.6 reshape.542
  335.2 267.3 %reduce-scatter.2.cloned.1.call-done = f32[48,24,384]{2,1,0:T(8,128)} async-done(((f32[48,384,384]{2,1,0:T(8,128)}), f32[48,24,384]{2,1,0:T(8,128)}) %reduce-scatter.2.cloned.1.call-update) | async-done | bytes 1769488 | tf_op jit(solution)/shard_map/reduce_scatter | solution.py:331
  605.1 37.6 %all-reduce.5.cloned.1.call-done = bf16[48,1,24,384]{3,2,0,1:T(8,128)(2,1)} async-done(((bf16[48,1,24,384]{3,2,0,1:T(8,128)(2,1)}), bf16[48,1,24,384]{3,2,0,1:T(8,128)(2,1)}) %all-reduce.5.cloned.1.call-update) | async-done | bytes 884752 | tf_op jit(solution)/shard_map/psum | solution.py:340
  657.2 9.7 copy.485
  666.9 12.9 fusion.17
  692.9 132.1 %all-to-all-done = bf16[16,3,7,24,384]{4,3,2,1,0:T(8,128)(2,1)} async-done(((bf16[16,3,7,24,384]{4,3,2,1,0:T(8,128)(2,1)}), bf16[16,3,7,24,384]{4,3,2,1,0:T(8,128)(2,1)}, u32[]{:S(2)}, u32[]{:S(2)}) %all-to-all-start) | async-done | bytes 6193184 | tf_op jit(solution)/shard_map/all_to_all | solution.py:359
  828.9 9.1 fusion.152
  870.3 36.8 %custom-call.32 = f32[3,128,128]{2,1,0:T(8,128)} custom-call(f32[3,128,128]{2,1,0:T(8,128)} %cholesky.322), custom_call_target="Cholesky" | custom-call | tf_op jit(solution)/shard_map/jit(cholesky)/cholesky | solution.py:122
  921.1 37.0 %custom-call.26 = f32[3,128,128]{2,1,0:T(8,128)} custom-call(f32[3,128,128]{2,1,0:T(8,128)} %cholesky.314), custom_call_target="Cholesky" | custom-call | tf_op jit(solution)/shard_map/jit(cholesky)/cholesky | solution.py:122
  961.2 30.9 %custom-call.33 = f32[3,1,128,128]{2,3,1,0:T(8,128)} custom-call(f32[3,1,128,128]{3,2,1,0:T(8,128)} %get-tuple-element.229), custom_call_target="InvertDiagBlocksLowerTriangular" | custom-call | tf_op jit(solution)/shard_map/jit(cholesky)/cholesky | solution.py:122
  997.4 36.6 %custom-call.34 = f32[3,128,128]{2,1,0:T(8,128)} custom-call(f32[3,128,128]{2,1,0:T(8,128)} %cholesky.326), custom_call_target="Cholesky" | custom-call | tf_op jit(solution)/shard_map/jit(cholesky)/cholesky | solution.py:122
  1036.2 31.1 %custom-call.27 = f32[3,1,128,128]{2,3,1,0:T(8,128)} custom-call(f32[3,1,128,128]{3,2,1,0:T(8,128)} %get-tuple-element.230), custom_call_target="InvertDiagBlocksLowerTriangular" | custom-call | tf_op jit(solution)/shard_map/jit(cholesky)/cholesky | solution.py:122
  1072.5 36.6 %custom-call.28 = f32[3,128,128]{2,1,0:T(8,128)} custom-call(f32[3,128,128]{2,1,0:T(8,128)} %cholesky.318), custom_call_target="Cholesky" | custom-call | tf_op jit(solution)/shard_map/jit(cholesky)/cholesky | solution.py:122
  1111.1 30.9 %custom-call.29 = f32[3,1,128,128]{2,3,1,0:T(8,128)} custom-call(f32[3,1,128,128]{3,2,1,0:T(8,128)} %get-tuple-element.228), custom_call_target="InvertDiagBlocksLowerTriangular" | custom-call | tf_op jit(solution)/shard_map/jit(cholesky)/cholesky | solution.py:122
  1146.5 36.8 %custom-call.30 = f32[3,128,128]{2,1,0:T(8,128)} custom-call(f32[3,128,128]{2,1,0:T(8,128)} %convolution_subtract_fusion.7), custom_call_target="Cholesky" | custom-call | tf_op jit(solution)/shard_map/jit(cholesky)/cholesky | solution.py:122
  1183.3 30.9 %custom-call.35 = f32[3,1,128,128]{2,3,1,0:T(8,128)} custom-call(f32[3,1,128,128]{3,2,1,0:T(8,128)} %get-tuple-element.213), custom_call_target="InvertDiagBlocksLowerTriangular" | custom-call | tf_op jit(solution)/shard_map/jit(cholesky)/cholesky | solution.py:122
  1218.6 36.6 %custom-call.36 = f32[3,128,128]{2,1,0:T(8,128)} custom-call(f32[3,128,128]{2,1,0:T(8,128)} %convolution_subtract_fusion.6), custom_call_target="Cholesky" | custom-call | tf_op jit(solution)/shard_map/jit(cholesky)/cholesky | solution.py:122
  1263.2 11.1 while.4
  1274.2 90.3 %custom-call.31 = f32[3,3,128,128]{2,3,1,0:T(8,128)} custom-call(f32[3,3,128,128]{3,2,1,0:T(8,128)} %bitcast.472), custom_call_target="InvertDiagBlocksLowerTriangular" | custom-call | tf_op jit(solution)/shard_map/vmap(jit(_solve_triangular))/triangular_solve | solution.py:125
  1378.9 9.1 while.5
  1388.0 88.6 %custom-call.37 = f32[3,3,128,128]{2,3,1,0:T(8,128)S(1)} custom-call(f32[3,3,128,128]{3,2,1,0:T(8,128)S(1)} %bitcast.471), custom_call_target="InvertDiagBlocksLowerTriangular" | custom-call | tf_op jit(solution)/shard_map/vmap(jit(_solve_triangular))/triangular_solve | solution.py:125
  1489.9 9.4 copy.378
  1506.4 189.1 %all-reduce.2 = bf16[9216]{0:T(1024)(128)(2,1)S(1)} all-reduce(f32[9216]{0:T(1024)S(1)} %reshape.551), channel_id=3, replica_groups=mesh['fsdp'=16,'dp'=2] {'fsdp'}, use_global_device_ids=true, to_apply=%region_30.33.clone | all-reduce | flops 9216 | bytes 55296
  1714.0 8.0 reshape.545
  (405 shorter events, 366.7 us)
Async XLA Ops:
  7.2 57.8 %all-gather.3.cloned.1.call-start = ((), (), s32[]{:S(2)}) async-start(), calls=%async_computation.3 | async-start | bytes 5013504 | tf_op jit(solution)/shard_map/all_gather | solution.py:191
  9.6 137.5 %all-gather.5.cloned.1.call-start = ((), (), s32[]{:S(2)}) async-start(), calls=%async_computation.4 | async-start | bytes 10027008 | tf_op jit(solution)/shard_map/all_gather | solution.py:221
  10.5 592.0 %reduce-scatter.2.cloned.1.call-start = ((), (), s32[]{:S(2)}) async-start(), calls=%async_computation.5 | async-start | bytes 30081024 | tf_op jit(solution)/shard_map/reduce_scatter | solution.py:331
  62.9 132.0 %copy-start.57 = (f32[512]{0:T(512)}, f32[512]{0:T(512)S(1)}, u32[]{:S(2)}) copy-start(f32[512]{0:T(512)S(1)} %fusion.134) | copy-start | bytes 6148
  77.3 10.6 copy-start.47
  196.7 8.1 copy-start.16
  196.7 51.5 %copy-start.68 = (f32[512]{0:T(512)}, f32[512]{0:T(512)S(1)}, u32[]{:S(2)}) copy-start(f32[512]{0:T(512)S(1)} %negate_multiply_fusion.2) | copy-start | bytes 6148
  209.1 31.7 %copy-start.70 = (f32[512]{0:T(512)}, f32[512]{0:T(512)S(1)}, u32[]{:S(2)}) copy-start(f32[512]{0:T(512)S(1)} %negate_multiply_fusion.1) | copy-start | bytes 6148
  213.4 16.7 slice-start
  213.4 16.7 slice-start.1
  220.9 33.0 %copy-start.49 = (bf16[12,64,512]{2,1,0:T(8,128)(2,1)}, bf16[12,64,512]{2,1,0:T(8,128)(2,1)S(1)}, u32[]{:S(2)}) copy-start(bf16[12,64,512]{2,1,0:T(8,128)(2,1)S(1)} %get-tuple-element.258) | copy-start | bytes 2359300
  220.9 9.3 slice-start.2
  239.0 14.9 copy-start.53
  240.8 13.1 copy-start.31
  313.6 13.0 slice-start.3
  313.6 13.0 slice-start.4
  335.2 307.5 %all-reduce.5.cloned.1.call-start = ((), (), s32[]{:S(2)}) async-start(), calls=%async_computation.6 | async-start | bytes 1769472 | tf_op jit(solution)/shard_map/psum | solution.py:340
  605.0 40.2 %copy-start.35 = (f32[48,24,384]{2,1,0:T(8,128)S(1)}, f32[48,24,384]{2,1,0:T(8,128)}, u32[]{:S(2)}) copy-start(f32[48,24,384]{2,1,0:T(8,128)} %param.20) | copy-start | bytes 5308420
  605.1 61.8 %copy-start.66 = (s32[48]{0:T(128)}, s32[48]{0:T(128)S(1)}, u32[]{:S(2)}) copy-start(s32[48]{0:T(128)S(1)} %fusion.122) | copy-start | bytes 580
  683.8 141.2 %all-to-all-start = ((bf16[16,3,7,24,384]{4,3,2,1,0:T(8,128)(2,1)}), bf16[16,3,7,24,384]{4,3,2,1,0:T(8,128)(2,1)}, u32[]{:S(2)}, u32[]{:S(2)}) async-start(bf16[16,3,7,24,384]{4,3,2,1,0:T(8,128)(2,1)} %copy.331), calls=%async_computation.1 | async-start | bytes 12386304 | tf_op jit(solution)/shard_map/all_to_all | solution.py:359
  838.0 12.4 slice-start.6
  840.0 8.5 copy-start.2
  843.2 7.2 slice-start.7
  866.1 42.3 %copy-start.1 = (f32[3,384,384]{2,1,0:T(8,128)S(1)}, f32[3,384,384]{2,1,0:T(8,128)}, u32[]{:S(2)}) copy-start(f32[3,384,384]{2,1,0:T(8,128)} %get-tuple-element.250) | copy-start | bytes 5308420
  1111.1 144.1 %copy-start.56 = (pred[128,128]{1,0:T(8,128)(4,1)S(1)}, pred[128,128]{1,0:T(8,128)(4,1)}, u32[]{:S(2)}) copy-start(pred[128,128]{1,0:T(8,128)(4,1)} %iota_compare_fusion.3) | copy-start | bytes 49156
  1499.4 207.8 %all-to-all-start.1 = ((bf16[1,3,7,384,384]{4,2,1,0,3:T(8,128)(2,1)}), bf16[1,3,7,384,384]{4,2,1,0,3:T(8,128)(2,1)}, u32[]{:S(2)}, u32[]{:S(2)}) async-start(bf16[1,3,7,384,384]{4,2,1,0,3:T(8,128)(2,1)} %copy.378), calls=%async_computation.2 | async-start | bytes 14155776 | tf_op jit(solution)/shard_map/all_to_all | solution.py:363
  1504.7 196.0 %copy-start.64 = (f32[576]{0:T(1024)S(1)}, f32[576]{0:T(1024)}, u32[]{:S(2)}) copy-start(f32[576]{0:T(1024)} %param.26) | copy-start | bytes 6916
  1504.7 196.0 %copy-start.74 = (f32[576]{0:T(1024)S(1)}, f32[576]{0:T(1024)}, u32[]{:S(2)}) copy-start(f32[576]{0:T(1024)} %param.28) | copy-start | bytes 6916
  1504.7 196.0 %copy-start.75 = (f32[576]{0:T(1024)S(1)}, f32[576]{0:T(1024)}, u32[]{:S(2)}) copy-start(f32[576]{0:T(1024)} %param.27) | copy-start | bytes 6916
  1504.7 196.6 %copy-start.32 = (bf16[12,64,512]{2,1,0:T(8,128)(2,1)S(1)}, bf16[12,64,512]{2,1,0:T(8,128)(2,1)}, u32[]{:S(2)}) copy-start(bf16[12,64,512]{2,1,0:T(8,128)(2,1)} %copy-done.31) | copy-start | bytes 2359300
  1504.7 196.6 %copy-start.71 = (f32[512]{0:T(512)S(1)}, f32[512]{0:T(512)}, u32[]{:S(2)}) copy-start(f32[512]{0:T(512)} %copy-done.70) | copy-start | bytes 6148
  1505.0 196.3 %copy-start.50 = (bf16[12,64,512]{2,1,0:T(8,128)(2,1)S(1)}, bf16[12,64,512]{2,1,0:T(8,128)(2,1)}, u32[]{:S(2)}) copy-start(bf16[12,64,512]{2,1,0:T(8,128)(2,1)} %copy-done.49) | copy-start | bytes 2359300
  (68 other events, 217.8 us)
Sparse Core Ops, SparseCore 0:
  10.8 54.1 all-gather.2
  67.7 79.3 all-gather.4
  335.3 267.1 reduce-scatter.1
  605.3 37.3 all-reduce.4
where the time goes:
time: 1780 us; the launch traced here: 1760 us
  other arithmetic  577 us (32%)
  waiting for transfers between devices  496 us (28%)
  local copies, waits for them, and re-layouts  246 us (14%)
  blocking collectives  244 us (14%)
  matrix products  167 us (9%)
    another operation x20, other arithmetic, orthonormal(): lower_factor = jnp.linalg.cholesky(gram_matrix)  350 us
    reduce_scatter x1, waiting for transfers between devices, shards(): lax.psum_scatter(jnp.concatenate([attn_blocks, ffn_blocks], axis=0), 'fsd...  267 us
    unnamed x2, blocking collectives  239 us
    another operation x5, other arithmetic, solve_one(): return jax.scipy.linalg.solve_triangular(factor, target, lower=True)  184 us
    all_to_all x1, waiting for transfers between devices, shards(): lax.all_to_all(outgoing.astype(jnp.bfloat16), 'fsdp', split_axis=0, conca...  132 us
    unnamed x220, local copies, waits for them, and re-layouts  75 us
    all_gather x1, waiting for transfers between devices, shards(): lax.all_gather(low_matrices[attn_end:], 'fsdp', axis=1, tiled=True)  56.8 us
    psum x1, waiting for transfers between devices, shards(): lax.psum(grad_share.astype(jnp.bfloat16), 'dp').astype(jnp.float32)  37.6 us
  transfers between devices with their start and end apart: 6, of which 5 were waited for; matrix products, arithmetic and copies ran while one was open for 2% of the time, Pallas kernels for 0%

commit v1 on v0

v1 whole, which is shorter than its diff:
```python
import functools

import jax
import jax.numpy as jnp
from jax import lax
from jax.experimental import pallas as pl
from jax.experimental.pallas import tpu as pltpu
from jax.sharding import PartitionSpec as P

F32 = jnp.float32
BF16 = jnp.bfloat16
MESH = pl.DeviceIdType.MESH

HEADS = 12
HEAD_DIM = 64
FF = 3072
ADAM_STEP = 10


FIRST_DECAY = 0.9
SECOND_DECAY = 0.999
STAT_DECAY = 0.95
ADAM_EPSILON = 1e-08
NORM_EPSILON = 1e-05
MATRIX_RATE = 0.03
VECTOR_RATE = 0.2
WEIGHT_DECAY = 0.01


def assemble(blocks, row_count, column_count):
    block_side = blocks.shape[-1]
    shaped = blocks.reshape(row_count, column_count, block_side, block_side)
    return shaped.transpose(0, 2, 1, 3).reshape(row_count * block_side, column_count * block_side)


def split_blocks(matrix, row_count, column_count, block_side):
    shaped = matrix.reshape(row_count, block_side, column_count, block_side)
    return shaped.transpose(0, 2, 1, 3).reshape(row_count * column_count, block_side, block_side)


def layer_norm(values, gain_row, shift_row):
    center = jnp.mean(values, axis=-1, keepdims=True)
    centered = values - center
    spread = jnp.mean(centered * centered, axis=-1, keepdims=True)
    return centered * lax.rsqrt(spread + NORM_EPSILON) * gain_row + shift_row


def exact_gelu(hidden):
    return jax.nn.gelu(hidden, approximate=False)


def masked_scores(heads_query, heads_key, length):
    slots = heads_query.shape[0]
    scores = jnp.einsum(
        "qhd,khd->hqk", heads_query, heads_key, preferred_element_type=jnp.float32
    ) * HEAD_DIM ** (-0.5)
    visible = lax.iota(jnp.int32, slots) < length
    return jnp.where(visible[None, None, :], scores, -1e30)


def attend(pieces):
    query_rows, key_rows, value_rows, length = pieces
    slots = query_rows.shape[0]
    heads_query = query_rows.reshape(slots, HEADS, HEAD_DIM)
    heads_key = key_rows.reshape(slots, HEADS, HEAD_DIM)
    heads_value = value_rows.reshape(slots, HEADS, HEAD_DIM)
    scores = masked_scores(heads_query, heads_key, length)
    row_max = jnp.max(scores, axis=-1, keepdims=True)
    shifted = jnp.exp(scores - row_max)
    row_total = jnp.sum(shifted, axis=-1, keepdims=True)
    attention_weights = (shifted / row_total).astype(jnp.bfloat16)
    context = jnp.einsum(
        "hqk,khd->qhd", attention_weights, heads_value, preferred_element_type=jnp.float32
    )
    return (
        context.reshape(slots, -1).astype(jnp.bfloat16),
        row_max[..., 0] + jnp.log(row_total[..., 0]),
    )


def attend_back(pieces):
    query_rows, key_rows, value_rows, logsum, grad_context, length = pieces
    slots = query_rows.shape[0]
    heads_query = query_rows.reshape(slots, HEADS, HEAD_DIM)
    heads_key = key_rows.reshape(slots, HEADS, HEAD_DIM)
    heads_value = value_rows.reshape(slots, HEADS, HEAD_DIM)
    heads_grad = grad_context.reshape(slots, HEADS, HEAD_DIM)
    scores = masked_scores(heads_query, heads_key, length)
    attention_weights = jnp.exp(scores - logsum[..., None])
    weights_low = attention_weights.astype(jnp.bfloat16)
    grad_values = jnp.einsum(
        "hqk,qhd->khd", weights_low, heads_grad, preferred_element_type=jnp.float32
    )
    grad_weights = jnp.einsum(
        "qhd,khd->hqk", heads_grad, heads_value, preferred_element_type=jnp.float32
    )
    grad_scores = attention_weights * (
        grad_weights - jnp.sum(grad_weights * attention_weights, axis=-1, keepdims=True)
    )
    scores_low = grad_scores.astype(jnp.bfloat16)
    grad_query = jnp.einsum(
        "hqk,khd->qhd", scores_low, heads_key, preferred_element_type=jnp.float32
    ) * HEAD_DIM ** (-0.5)
    grad_keys = jnp.einsum(
        "hqk,qhd->khd", scores_low, heads_query, preferred_element_type=jnp.float32
    ) * HEAD_DIM ** (-0.5)
    return (
        grad_query.reshape(slots, -1).astype(jnp.bfloat16),
        grad_keys.reshape(slots, -1).astype(jnp.bfloat16),
        grad_values.reshape(slots, -1).astype(jnp.bfloat16),
    )


def dg(a,b,ca,cb):
    return lax.dot_general(a,b,(((ca,),(cb,)),((),())),preferred_element_type=F32)

def halves(a):
    hi=a.astype(BF16)
    return hi,(a-hi.astype(F32)).astype(BF16)

def mm3(a,b,ca,cb):
    ah,al=halves(a); bh,bl=halves(b)
    return dg(ah,bh,ca,cb)+(dg(ah,bl,ca,cb)+dg(al,bh,ca,cb))

def thirds(u):
    h=u.astype(BF16).astype(F32); r=u-h
    m=r.astype(BF16).astype(F32)
    return h,m,r-m

def factor_panels(aug, slots, side=128):
    sub=lax.broadcasted_iota(jnp.int32,(8,side),0)
    def spread(v): return jnp.broadcast_to(v,(8,side))
    for p in range(side//8):
        k=8*p
        panels=[]
        for s in range(slots):
            pw=aug[s,k:k+8,:side]; pv=aug[s,k:k+8,side:]
            cols=[spread(pw[:,k+i:k+i+1]) for i in range(8)]
            S=[[spread(cols[i][j:j+1,:]) if j>=i else None for i in range(8)] for j in range(8)]
            rw=[spread(pw[i:i+1,:]) for i in range(8)]
            rv=[spread(pv[i:i+1,:]) for i in range(8)]
            panels.append((S,rw,rv))
        for i in range(8):
            for S,rw,rv in panels:
                r=lax.rsqrt(S[i][i])
                for j in range(i+1,8): S[j][i]=S[j][i]*r
                for m in range(i+1,8):
                    for j in range(m,8):
                        S[j][m]=S[j][m]-S[j][i]*S[m][i]
                rw[i]=rw[i]*r; rv[i]=rv[i]*r
                for j in range(i+1,8):
                    rw[j]=rw[j]-S[j][i]*rw[i]
                    rv[j]=rv[j]-S[j][i]*rv[i]
        for s,(S,rw,rv) in enumerate(panels):
            uw,uv=rw[0],rv[0]
            for i in range(1,8):
                uw=jnp.where(sub==i,rw[i],uw); uv=jnp.where(sub==i,rv[i],uv)
            aug[s,k:k+8,side:]=uv
            if k+8<side:
                h,m,l=thirds(uw); vh,vm,vl=thirds(uv)
                a=jnp.concatenate([h,h,m,m,h,l],0).astype(BF16)
                b=jnp.concatenate([jnp.concatenate([h,m,h,m,l,h],0),jnp.concatenate([vh,vm,vh,vm,vl,vh],0)],1).astype(BF16)
                t=dg(a,b,0,0)
                aug[s,k+8:,:]=aug[s,k+8:,:]-t[k+8:,:]

def orthonormal_cols(mat, aug, slots, side=128):
    n=mat.shape[-1]
    r=lax.broadcasted_iota(jnp.int32,(side,side),0); c=lax.broadcasted_iota(jnp.int32,(side,side),1)
    eye=(r==c).astype(F32)
    steps=n//side
    for o in range(steps):
        lo=o*side
        for s in range(slots):
            mo=mat[s,:,lo:lo+side]
            aug[s,:,:side]=mm3(mo,mo,0,0)
            aug[s,:,side:]=eye
        factor_panels(aug,slots,side)
        for s in range(slots):
            q=mm3(mat[s,:,lo:lo+side],aug[s,:,side:],1,1)
            mat[s,:,lo:lo+side]=q
            if o+1<steps:
                rest=mat[s,:,lo+side:]
                mat[s,:,lo+side:]=rest-mm3(q,mm3(q,rest,0,0),1,0)


def soap_kernel(grad, stat, own, other, first, second, outer_out, basis_out, turned_out, update_out, mat, aug):
    slots = grad.shape[0]
    right_side = lax.rem(lax.axis_index("dp"), 2) == 1

    def run(is_right):
        near, far = (0, 1) if is_right else (1, 0)

        def one(s, carry):
            g = grad[s].astype(BF16)
            outer = dg(g, g, near, near)
            outer_out[s] = outer.astype(BF16)
            mixed = STAT_DECAY * stat[s].astype(F32) + (1.0 - STAT_DECAY) * outer
            high, rest = halves(mixed)
            mat[s] = dg(high, own[s], 1, 0) + dg(rest, own[s], 1, 0)
            left, right = (other[s], own[s]) if is_right else (own[s], other[s])
            rotated = dg(dg(left, g, 0, 0).astype(BF16), right, 1, 0)
            turned_out[s] = rotated.astype(BF16)
            first_new = FIRST_DECAY * first[s].astype(F32) + (1.0 - FIRST_DECAY) * rotated
            second_new = SECOND_DECAY * second[s].astype(F32) + (1.0 - SECOND_DECAY) * rotated * rotated
            direction = (
                first_new
                / (1.0 - FIRST_DECAY**ADAM_STEP)
                / (jnp.sqrt(second_new / (1.0 - SECOND_DECAY**ADAM_STEP)) + ADAM_EPSILON)
            )
            back = dg(left, direction.astype(BF16), 1, 0).astype(BF16)
            update_out[s] = dg(back, right, 1, 1).astype(BF16)
            return carry

        lax.fori_loop(0, slots, one, 0)

    @pl.when(right_side)
    def _():
        run(True)

    @pl.when(jnp.logical_not(right_side))
    def _():
        run(False)

    orthonormal_cols(mat, aug, slots)
    basis_out[...] = mat[...].astype(BF16)


def soap_blocks(grad, stat, own, other, first, second):
    slots, side, _ = grad.shape
    shape = jax.ShapeDtypeStruct(grad.shape, BF16)
    whole = pl.BlockSpec(memory_space=pltpu.VMEM)
    return pl.pallas_call(
        soap_kernel,
        out_shape=[shape] * 4,
        in_specs=[whole] * 6,
        out_specs=[whole] * 4,
        scratch_shapes=[
            pltpu.VMEM((slots, side, side), F32),
            pltpu.VMEM((slots, 128, 256), F32),
        ],
        compiler_params=pltpu.CompilerParams(vmem_limit_bytes=48 * 2**20),
        name="soap_blocks",
    )(grad, stat, own, other, first, second)


def ring_place(chip, chips):
    along, across = chip // 2, lax.rem(chip, 2)
    return along * (1 - across) + (chips - 1 - along) * across


def ring_chip(place, chips):
    place = lax.rem(place + 8 * chips, chips)
    across = place // (chips // 2)
    along = place * (1 - across) + (chips - 1 - place) * across
    return 2 * along + across


def whereabouts(chips):
    device, replica = lax.axis_index("fsdp"), lax.axis_index("dp")
    chip, core = device // 2, lax.rem(device, 2)
    place = ring_place(chip, chips)
    turn = 1 - 2 * core
    after = (2 * ring_chip(place + turn, chips) + core, replica)
    before = (2 * ring_chip(place - turn, chips) + core, replica)
    sibling = (2 * chip + 1 - core, replica)
    return device, replica, chip, core, place, turn, after, before, sibling


def greet(neighbours):
    barrier = pltpu.get_barrier_semaphore()
    for neighbour in neighbours:
        pl.semaphore_signal(barrier, inc=1, device_id=neighbour, device_id_type=MESH)
    pl.semaphore_wait(barrier, len(neighbours))


def gather_kernel(chips, share, mat_ref, vec_ref, attn, up, down, vecs, raw_a, raw_u, raw_d, low_a, low_u, low_d,
                  low_v, trade_send, trade_recv, own_sem, ring_send, ring_recv, sib_send, sib_recv):
    device, replica, chip, core, place, turn, after, before, sibling = whereabouts(chips)
    side = mat_ref.shape[-1]
    wide = attn.shape[-1] // 2
    slim = down.shape[-1] // 2
    both = 2 * share
    rows = pl.ds(pl.multiple_of(share * core, 8), share)
    for b in range(16):
        raw_a[(b % 4) // 2, rows, (b // 4) * 2 * side + (b % 2) * side : (b // 4) * 2 * side + (b % 2 + 1) * side] = mat_ref[b]
        raw_u[b // 8, rows, (b % 8) * side : (b % 8 + 1) * side] = mat_ref[16 + b]
        raw_d[b // 2, rows, (b % 2) * side : (b % 2 + 1) * side] = mat_ref[32 + b]
    low_v[...] = vec_ref[...].astype(BF16).astype(F32)
    greet((after, before, sibling))
    groups = ((raw_a, low_a, attn, wide), (raw_u, low_u, up, wide), (raw_d, low_d, down, slim))

    def half(which, width):
        return pl.ds(pl.multiple_of(which * width, 128), width)

    trades = []
    for g, (raw, low, out, width) in enumerate(groups):
        part = raw.at[:, rows, half(1 - core, width)]
        trade = pltpu.make_async_remote_copy(
            src_ref=part, dst_ref=part, send_sem=trade_send.at[g], recv_sem=trade_recv.at[g],
            device_id=sibling, device_id_type=MESH)
        trade.start()
        trades.append(trade)

    def slab(g, origin):
        raw, low, out, width = groups[g]
        return out.at[:, pl.ds(pl.multiple_of(origin * both, 16), both), half(core, width)]

    def vec_of(origin):
        return vecs.at[2 * origin + core]

    def piece(g, origin):
        return vec_of(origin) if g == 3 else slab(g, origin)

    def forward(g, t, origin, source):
        return pltpu.make_async_remote_copy(
            src_ref=source, dst_ref=piece(g, origin), send_sem=ring_send.at[t, g], recv_sem=ring_recv.at[t, g],
            device_id=after, device_id_type=MESH)

    def pass_on(g, t, origin, source):
        return pltpu.make_async_remote_copy(
            src_ref=source, dst_ref=piece(g, origin), send_sem=sib_send.at[t, g], recv_sem=sib_recv.at[t, g],
            device_id=sibling, device_id_type=MESH)

    sources = [low_a, low_u, low_d, low_v]
    owns = []
    for g in (3, 0, 1, 2):
        if g < 3:
            raw, low, out, width = groups[g]
            trades[g].wait()
            low[...] = raw[:, :, half(core, width)].astype(BF16)
        forward(g, 0, chip, sources[g]).start()
        pass_on(g, 0, chip, sources[g]).start()
        own = pltpu.make_async_copy(sources[g], piece(g, chip), own_sem.at[g])
        own.start()
        owns.append(own)

    def step(t, carry):
        origin = ring_chip(place - turn * t, chips)
        for g in (3, 0, 1, 2):
            arrived = piece(g, origin)
            forward(g, t - 1, origin, arrived).wait_recv()

            @pl.when(t < chips - 1)
            def _():
                forward(g, t, origin, arrived).start()

            pass_on(g, t, origin, arrived).start()
        return carry

    lax.fori_loop(1, chips, step, 0)
    for own in owns:
        own.wait()

    def finish(t, carry):
        for g in range(4):
            @pl.when(t < chips - 1)
            def _():
                forward(g, t, chip, piece(g, chip)).wait_send()

            pass_on(g, t, chip, piece(g, chip)).wait()
        return carry

    lax.fori_loop(0, chips, finish, 0)


def gather_weights(matrices, vector_tile, chips):
    total, share, side = matrices.shape
    both = 2 * share
    anywhere = pl.BlockSpec(memory_space=pl.ANY)
    whole = pl.BlockSpec(memory_space=pltpu.VMEM)
    dma = pltpu.SemaphoreType.DMA
    return pl.pallas_call(
        functools.partial(gather_kernel, chips, share),
        out_shape=[
            jax.ShapeDtypeStruct((2, side, 8 * side), BF16),
            jax.ShapeDtypeStruct((2, side, 8 * side), BF16),
            jax.ShapeDtypeStruct((8, side, 2 * side), BF16),
            jax.ShapeDtypeStruct((2 * chips, 8, 128), F32),
        ],
        in_specs=[whole, whole],
        out_specs=[anywhere] * 4,
        scratch_shapes=[
            pltpu.VMEM((2, both, 8 * side), F32),
            pltpu.VMEM((2, both, 8 * side), F32),
            pltpu.VMEM((8, both, 2 * side), F32),
            pltpu.VMEM((2, both, 4 * side), BF16),
            pltpu.VMEM((2, both, 4 * side), BF16),
            pltpu.VMEM((8, both, side), BF16),
            pltpu.VMEM((8, 128), F32),
            dma((3,)), dma((3,)), dma((4,)),
            dma((chips - 1, 4)), dma((chips - 1, 4)), dma((chips, 4)), dma((chips, 4)),
        ],
        compiler_params=pltpu.CompilerParams(collective_id=1, has_side_effects=True, vmem_limit_bytes=40 * 2**20),
        name="gather_weights",
    )(matrices, vector_tile)


def reduce_kernel(chips, g_qkv, g_out, g_up, g_down, g_vec, owned, vec_sum, mine, theirs, ring, peer, vmine, vring, vpeer,
                  mine_sem, sib_send, sib_recv, ring_send, ring_recv, peer_send, peer_recv):
    device, replica, chip, core, place, turn, after, before, sibling = whereabouts(chips)
    other = (device, 1 - replica)
    side = mine.shape[-1]
    greet((after, before, sibling, other))

    def column(index):
        return pl.ds(pl.multiple_of(index * side, 128), side)

    def fetch(owner, start):
        which = owner // 4
        i, j = lax.rem(owner, 4) // 2, lax.rem(owner, 2)

        @pl.when(which < 3)
        def _():
            start(0, g_qkv.at[i, :, column(2 * which + j)])

        @pl.when(which == 3)
        def _():
            start(0, g_out.at[i, :, column(j)])

        start(1, g_up.at[owner // 8, :, column(lax.rem(owner, 8))])
        start(2, g_down.at[owner // 2, :, column(lax.rem(owner, 2))])
        start(3, g_vec.at[owner])

    def local(t, slot, source):
        target = vmine.at[0, t] if slot == 3 else mine.at[t, slot]
        return pltpu.make_async_copy(source, target, mine_sem.at[t, slot])

    def to_sibling(t, slot, source):
        target = vmine.at[1, t] if slot == 3 else theirs.at[t, slot]
        return pltpu.make_async_remote_copy(
            src_ref=source, dst_ref=target, send_sem=sib_send.at[t, slot], recv_sem=sib_recv.at[t, slot],
            device_id=sibling, device_id_type=MESH)

    def to_next(t, slot):
        source, target = (vmine.at[0, t], vring.at[t]) if slot == 3 else (mine.at[t, slot], ring.at[t, slot])
        return pltpu.make_async_remote_copy(
            src_ref=source, dst_ref=target, send_sem=ring_send.at[t, slot], recv_sem=ring_recv.at[t, slot],
            device_id=after, device_id_type=MESH)

    def to_other(slot):
        source, target = (vmine.at[0, chips - 1], vpeer) if slot == 3 else (mine.at[chips - 1, slot], peer.at[slot])
        return pltpu.make_async_remote_copy(
            src_ref=source, dst_ref=target, send_sem=peer_send.at[slot], recv_sem=peer_recv.at[slot],
            device_id=other, device_id_type=MESH)

    def begin(t, carry):
        fetch(2 * ring_chip(place + turn * (t + 1), chips) + 1 - core, lambda slot, source: to_sibling(t, slot, source).start())
        fetch(2 * ring_chip(place - turn * (t + 1), chips) + core, lambda slot, source: local(t, slot, source).start())
        return carry

    lax.fori_loop(0, chips, begin, 0)

    def sources(slot):
        return g_vec.at[0] if slot == 3 else g_up.at[0, :, :side]

    def ready(t, slot):
        local(t, slot, sources(slot)).wait()
        to_sibling(t, slot, sources(slot)).wait_recv()

    for slot in (3, 0, 1, 2):
        ready(0, slot)
        if slot == 3:
            vmine[0, 0] = vmine[0, 0] + vmine[1, 0]
        else:
            mine[0, slot] = (mine[0, slot].astype(F32) + theirs[0, slot].astype(F32)).astype(BF16)
        to_next(0, slot).start()

    def step(t, carry):
        for slot in (3, 0, 1, 2):
            ready(t, slot)
            to_next(t - 1, slot).wait_recv()
            if slot == 3:
                vmine[0, t] = vmine[0, t] + vmine[1, t] + vring[t - 1]
            else:
                total = mine[t, slot].astype(F32) + theirs[t, slot].astype(F32) + ring[t - 1, slot].astype(F32)
                mine[t, slot] = total.astype(BF16)

            @pl.when(t < chips - 1)
            def _():
                to_next(t, slot).start()

            @pl.when(t == chips - 1)
            def _():
                to_other(slot).start()
        return carry

    lax.fori_loop(1, chips, step, 0)
    for slot in (3, 0, 1, 2):
        to_other(slot).wait()
        if slot == 3:
            vec_sum[...] = vmine[0, chips - 1] + vpeer[...]
        else:
            owned[slot] = (mine[chips - 1, slot].astype(F32) + peer[slot].astype(F32)).astype(BF16)

    def finish(t, carry):
        for slot in range(4):
            to_sibling(t, slot, sources(slot)).wait_send()

            @pl.when(t < chips - 1)
            def _():
                to_next(t, slot).wait_send()
        return carry

    lax.fori_loop(0, chips, finish, 0)


def reduce_gradients(g_qkv, g_out, g_up, g_down, g_vec, chips):
    side = g_up.shape[1]
    anywhere = pl.BlockSpec(memory_space=pl.ANY)
    whole = pl.BlockSpec(memory_space=pltpu.VMEM)
    dma = pltpu.SemaphoreType.DMA
    return pl.pallas_call(
        functools.partial(reduce_kernel, chips),
        out_shape=[jax.ShapeDtypeStruct((3, side, side), BF16), jax.ShapeDtypeStruct((8, 128), F32)],
        in_specs=[anywhere] * 5,
        out_specs=[whole] * 2,
        scratch_shapes=[
            pltpu.VMEM((chips, 3, side, side), BF16),
            pltpu.VMEM((chips, 3, side, side), BF16),
            pltpu.VMEM((chips - 1, 3, side, side), BF16),
            pltpu.VMEM((3, side, side), BF16),
            pltpu.VMEM((2, chips, 8, 128), F32),
            pltpu.VMEM((chips - 1, 8, 128), F32),
            pltpu.VMEM((8, 128), F32),
            dma((chips, 4)), dma((chips, 4)), dma((chips, 4)),
            dma((chips - 1, 4)), dma((chips - 1, 4)), dma((4,)), dma((4,)),
        ],
        compiler_params=pltpu.CompilerParams(collective_id=2, has_side_effects=True, vmem_limit_bytes=48 * 2**20),
        name="reduce_gradients",
    )(g_qkv, g_out, g_up, g_down, g_vec)


def plain_gather(matrices, vectors):
    side = matrices.shape[-1]
    blocks = lax.all_gather(matrices.astype(BF16), "fsdp", axis=1, tiled=True)
    attn = jnp.concatenate([assemble(blocks[4 * part : 4 * part + 4], 2, 2) for part in range(4)], axis=1)
    up = assemble(blocks[16:32], 2, 8)
    down = assemble(blocks[32:], 8, 2)
    rows = lax.all_gather(vectors.astype(BF16), "fsdp", axis=0, tiled=True)
    return attn, up, down, rows.astype(F32).reshape(-1, 2 * side)


def plain_reduce(grad_qkv, grad_out, grad_up, grad_down, vector_grad, capacity):
    shard_count = lax.axis_size("fsdp")
    width = grad_up.shape[0]
    side = width // 2
    blocks = jnp.concatenate(
        [split_blocks(grad_qkv[:, part * width : (part + 1) * width], 2, 2, side) for part in range(3)]
        + [split_blocks(grad_out, 2, 2, side), split_blocks(grad_up, 2, 8, side), split_blocks(grad_down, 8, 2, side)],
        axis=0,
    )
    owned = lax.psum_scatter(
        to_owners(blocks, capacity, shard_count), "fsdp", scatter_dimension=1, tiled=True
    )
    owned = lax.psum(owned, "dp")[:, 0]
    share = lax.psum_scatter(vector_grad, "fsdp", scatter_dimension=0, tiled=True)
    return owned, lax.psum(share, "dp")


def to_owners(blocks, capacity, shard_count):
    spare = capacity * shard_count - blocks.shape[0]
    blocks = jnp.pad(blocks, ((0, spare),) + ((0, 0),) * (blocks.ndim - 1))
    return blocks.reshape((capacity, shard_count) + blocks.shape[1:])


def shards(
    tokens,
    cotangent,
    lengths,
    matrices,
    first_moment,
    second_moment,
    left_stat,
    right_stat,
    left_basis,
    right_basis,
    vectors,
    vector_first,
    vector_second,
):
    shard_count = lax.axis_size("fsdp")
    replicas = lax.axis_size("dp")
    sequences, slots, model_width = tokens.shape
    block_total, share_rows, block_side = matrices.shape
    unit_ratio = FF // model_width
    rows_total = sequences * slots
    capacity = -(-block_total // shard_count)
    ringed = replicas == 2 and capacity * shard_count == block_total == 48 and share_rows % 8 == 0 and capacity == 3
    vector_share = vectors.shape[0]

    def shaped(array):
        return array.reshape(sequences, slots, array.shape[-1])

    right_side = lax.axis_index("dp") % 2 == 1
    chosen = [
        jnp.where(right_side, right_stat, left_stat),
        jnp.where(right_side, right_basis, left_basis),
        jnp.where(right_side, left_basis, right_basis),
        first_moment,
        second_moment,
    ]
    states = jnp.stack([to_owners(part.astype(BF16), capacity, shard_count) for part in chosen])
    states = lax.all_to_all(states, "fsdp", split_axis=2, concat_axis=3, tiled=True)[:, :, 0]

    if ringed:
        vector_tile = jnp.pad(vectors, (0, 1024 - vector_share)).reshape(8, 128)
        attn, up, down, vector_tiles = gather_weights(matrices, vector_tile, shard_count // 2)
        attn = attn.reshape(model_width, 4 * model_width)
        up = up.reshape(model_width, FF)
        down = down.reshape(FF, model_width)
        vector_rows = vector_tiles.reshape(shard_count, 1024)[:, :vector_share].reshape(-1, model_width)
    else:
        attn, up, down, vector_rows = plain_gather(matrices, vectors)
    weight_qkv, weight_out = attn[:, : 3 * model_width], attn[:, 3 * model_width :]
    inputs = tokens.reshape(rows_total, model_width)
    joined = jnp.dot(inputs, weight_qkv, preferred_element_type=F32)
    query_rows = (joined[:, :model_width] + vector_rows[0]).astype(BF16)
    key_rows = joined[:, model_width : 2 * model_width].astype(BF16)
    value_rows = (joined[:, 2 * model_width :] + vector_rows[1]).astype(BF16)
    context, logsum = lax.map(
        attend, (shaped(query_rows), shaped(key_rows), shaped(value_rows), lengths)
    )
    context = context.reshape(rows_total, model_width)
    attended = jnp.dot(context, weight_out, preferred_element_type=F32) + vector_rows[2]
    normed, pull_one = jax.vjp(
        layer_norm, inputs.astype(F32) + attended, vector_rows[3], vector_rows[4]
    )
    normed_low = normed.astype(BF16)
    hidden = jnp.dot(normed_low, up, preferred_element_type=F32) + vector_rows[
        5 : 5 + unit_ratio
    ].reshape(FF)
    active, pull_gelu = jax.vjp(exact_gelu, hidden)
    active_low = active.astype(BF16)
    result = jnp.dot(active_low, down, preferred_element_type=F32) + vector_rows[5 + unit_ratio]
    output, pull_two = jax.vjp(
        layer_norm, normed + result, vector_rows[6 + unit_ratio], vector_rows[7 + unit_ratio]
    )
    block_out = output.reshape(sequences, slots, model_width).astype(BF16)
    visible = (lax.iota(jnp.int32, slots)[None, :] < lengths[:, None]).astype(F32)
    grad_output = (cotangent.astype(F32) * visible[:, :, None]).reshape(rows_total, model_width)
    grad_second, grad_gain_two, grad_shift_two = pull_two(grad_output)
    second_low = grad_second.astype(BF16)
    grad_down = jnp.einsum("tf,td->fd", active_low, second_low, preferred_element_type=F32)
    grad_active = jnp.einsum("td,fd->tf", second_low, down, preferred_element_type=F32)
    (grad_hidden,) = pull_gelu(grad_active)
    hidden_low = grad_hidden.astype(BF16)
    grad_up = jnp.einsum("td,tf->df", normed_low, hidden_low, preferred_element_type=F32)
    grad_normed = grad_second + jnp.einsum("tf,df->td", hidden_low, up, preferred_element_type=F32)
    grad_mixed, grad_gain_one, grad_shift_one = pull_one(grad_normed)
    mixed_low = grad_mixed.astype(BF16)
    grad_out_weight = jnp.einsum("td,te->de", context, mixed_low, preferred_element_type=F32)
    grad_context = jnp.einsum(
        "te,de->td", mixed_low, weight_out, preferred_element_type=F32
    ).astype(BF16)
    grad_query, grad_keys, grad_values = lax.map(
        attend_back,
        (
            shaped(query_rows),
            shaped(key_rows),
            shaped(value_rows),
            logsum,
            shaped(grad_context),
            lengths,
        ),
    )
    grad_joined = jnp.concatenate(
        [
            grad_query.reshape(rows_total, model_width),
            grad_keys.reshape(rows_total, model_width),
            grad_values.reshape(rows_total, model_width),
        ],
        axis=1,
    )
    grad_qkv = jnp.einsum("td,te->de", inputs, grad_joined, preferred_element_type=F32)
    input_grad = grad_mixed + jnp.einsum(
        "te,de->td", grad_joined, weight_qkv, preferred_element_type=F32
    )
    vector_grad = jnp.concatenate(
        [
            jnp.sum(grad_joined[:, :model_width], axis=0, dtype=F32)[None],
            jnp.sum(grad_joined[:, 2 * model_width :], axis=0, dtype=F32)[None],
            jnp.sum(grad_mixed, axis=0)[None],
            grad_gain_one[None],
            grad_shift_one[None],
            jnp.sum(grad_hidden, axis=0).reshape(unit_ratio, model_width),
            jnp.sum(grad_second, axis=0)[None],
            grad_gain_two[None],
            grad_shift_two[None],
        ],
        axis=0,
    ).reshape(-1)
    weight_grads = [part.astype(BF16) for part in (grad_qkv, grad_out_weight, grad_up, grad_down)]
    if ringed:
        tiles = jnp.pad(
            vector_grad.reshape(shard_count, vector_share), ((0, 0), (0, 1024 - vector_share))
        ).reshape(shard_count, 8, 128)
        slabs = [part.reshape(-1, block_side, part.shape[1]) for part in weight_grads]
        owned, vector_sum = reduce_gradients(*slabs, tiles, shard_count // 2)
        vector_sum = vector_sum.reshape(1024)[:vector_share]
    else:
        owned, vector_sum = plain_reduce(*weight_grads, vector_grad, capacity)
    filler = (lax.iota(jnp.int32, capacity) * shard_count + lax.axis_index("fsdp")) >= block_total
    stat = jnp.where(
        filler[:, None, None], jnp.eye(block_side, dtype=jnp.bfloat16), states[0]
    )
    basis = jnp.where(
        filler[:, None, None], jnp.eye(block_side, dtype=jnp.bfloat16), states[1]
    )
    outer, new_basis, turned, update = soap_blocks(
        owned, stat, basis, states[2], states[3], states[4]
    )
    returned = lax.all_to_all(
        jnp.stack([outer, new_basis, turned, update])[:, :, None],
        "fsdp",
        split_axis=3,
        concat_axis=2,
        tiled=True,
    ).reshape(4, capacity * shard_count, -1, block_side)[:, :block_total]
    mirror = lax.ppermute(
        returned[:2], "dp", [(place, place ^ 1) for place in range(lax.axis_size("dp"))]
    )
    returned = returned.astype(jnp.float32)
    mirror = mirror.astype(jnp.float32)
    left_pair = jnp.where(right_side, mirror, returned[:2])
    right_pair = jnp.where(right_side, returned[:2], mirror)
    turned = returned[2]
    local = [
        returned[3],
        FIRST_DECAY * first_moment + (1.0 - FIRST_DECAY) * turned,
        SECOND_DECAY * second_moment + (1.0 - SECOND_DECAY) * turned * turned,
        STAT_DECAY * left_stat + (1.0 - STAT_DECAY) * left_pair[0],
        STAT_DECAY * right_stat + (1.0 - STAT_DECAY) * right_pair[0],
        left_pair[1],
        right_pair[1],
    ]
    new_matrices = matrices - MATRIX_RATE * (local[0] + WEIGHT_DECAY * matrices)
    vfirst_new = FIRST_DECAY * vector_first + (1.0 - FIRST_DECAY) * vector_sum
    vsecond_new = SECOND_DECAY * vector_second + (1.0 - SECOND_DECAY) * vector_sum * vector_sum
    vector_new = vectors - VECTOR_RATE * (vfirst_new / (1.0 - FIRST_DECAY**ADAM_STEP)) / (
        jnp.sqrt(vsecond_new / (1.0 - SECOND_DECAY**ADAM_STEP)) + ADAM_EPSILON
    )
    return (
        block_out,
        input_grad.reshape(sequences, slots, model_width),
        new_matrices,
        new_matrices.astype(jnp.bfloat16),
        local[1],
        local[2],
        local[3],
        local[4],
        local[5],
        local[6],
        vfirst_new,
        vsecond_new,
        vector_new,
    )


def solution(mesh):
    return jax.shard_map(
        shards,
        mesh=mesh,
        in_specs=(
            P(("fsdp", "dp"), None, None),
            P(("fsdp", "dp"), None, None),
            P(("fsdp", "dp")),
            P(None, "fsdp", None),
            P(None, "fsdp", None),
            P(None, "fsdp", None),
            P(None, "fsdp", None),
            P(None, "fsdp", None),
            P(None, "fsdp", None),
            P(None, "fsdp", None),
            P("fsdp"),
            P("fsdp"),
            P("fsdp"),
        ),
        out_specs=(
            P(("fsdp", "dp"), None, None),
            P(("fsdp", "dp"), None, None),
            P(None, "fsdp", None),
            P(None, "fsdp", None),
            P(None, "fsdp", None),
            P(None, "fsdp", None),
            P(None, "fsdp", None),
            P(None, "fsdp", None),
            P(None, "fsdp", None),
            P(None, "fsdp", None),
            P("fsdp"),
            P("fsdp"),
            P("fsdp"),
        ),
        check_vma=False,
    )
```

time: 1780 us -> 585 us (0.33)
  other arithmetic: 577 us -> 36 us
  waiting for transfers between devices: 496 us -> 100 us
  Pallas kernels: 0 us -> 288 us
  blocking collectives: 244 us -> 0 us
  local copies, waits for them, and re-layouts: 246 us -> 39 us
  matrix products: 167 us -> 102 us
    another operation x27 -> x0, other arithmetic: 538 us -> none  [the longest x20 350 us: orthonormal(): lower_factor = jnp.linalg.cholesky(gram_matrix)]
    pallas_call x0 -> x3, Pallas kernels: none -> 288 us  [the longest x1 167 us: gather_weights(): pl.pallas_call(functools.partial(gather_kernel, chips, share), out_shape=...]
    reduce_scatter x1 -> x0, waiting for transfers between devices: 267 us -> none  [shards(): lax.psum_scatter(jnp.concatenate([attn_blocks, ffn_blocks], axis=0), 'fsd...]
    unnamed x2 -> x0, blocking collectives: 239 us -> none
    all_to_all x2, waiting for transfers between devices: 132 us -> 72.1 us  [the longest x1 72.1 us: shards(): lax.all_to_all(jnp.stack([outer, new_basis, turned, update])[:, :, None],...]
    unnamed x220 -> x100, local copies, waits for them, and re-layouts: 75 us -> 15.8 us
    all_gather x2 -> x0, waiting for transfers between devices: 58.8 us -> none  [the longest x1 56.8 us: shards(): lax.all_gather(low_matrices[attn_end:], 'fsdp', axis=1, tiled=True)]
    another operation x34 -> x3, local copies, waits for them, and re-layouts: 53.1 us -> 2.74 us  [the longest x2 2.65 us: shards(): jnp.stack([to_owners(part.astype(BF16), capacity, shard_count) for part i...]
  transfers between devices with their start and end apart: 6 -> 3, of which waited for: 5 -> 2; matrix products, arithmetic and copies ran while one was open for 2% -> 23% of each run, Pallas kernels for 0% -> 44%
where the time goes in v1:
time: 585 us; the launch traced here: 582 us
  Pallas kernels  288 us (49%)
  matrix products  102 us (17%)
  waiting for transfers between devices  100 us (17%)
  local copies, waits for them, and re-layouts  39 us (7%)
  other arithmetic  36 us (6%)
  starting transfers between devices  13.7 us (2%)
    pallas_call x1, Pallas kernels, gather_weights(): pl.pallas_call(functools.partial(gather_kernel, chips, share), out_shape=...  167 us
    pallas_call x1, Pallas kernels, reduce_gradients(): pl.pallas_call(functools.partial(reduce_kernel, chips), out_shape=[jax.Sh...  88.4 us
    all_to_all x1, waiting for transfers between devices, shards(): lax.all_to_all(jnp.stack([outer, new_basis, turned, update])[:, :, None],...  72.1 us
    pallas_call x1, Pallas kernels, soap_blocks(): pl.pallas_call(soap_kernel, out_shape=[shape] * 4, in_specs=[whole] * 6,...  32.7 us
    ppermute x1, waiting for transfers between devices, shards(): lax.ppermute(returned[:2], 'dp', [(place, place ^ 1) for place in range(l...  28 us
    dot_general x1, matrix products, shards(): jnp.dot(normed_low, up, preferred_element_type=F32)  18.5 us
    unnamed x100, local copies, waits for them, and re-layouts  15.8 us
  transfers between devices with their start and end apart: 3, of which 2 were waited for; matrix products, arithmetic and copies ran while one was open for 23% of the time, Pallas kernels for 44%

profile of v1, /device:TPU:12, one launch (start us, length us, event | category | flops | bytes accessed | tf_op | source)
XLA Modules:
  0.0 581.8 jit_solution(5294761042770197485)
XLA Ops:
  0.7 3.1 select_convert_fusion
  6.1 2.5 copy.67
  8.6 7.2 %all-to-all-start = ((bf16[5,3,16,24,384]{4,3,1,0,2:T(8,128)(2,1)}), bf16[5,3,16,24,384]{4,3,1,0,2:T(8,128)(2,1)}, u32[]{:S(2)}, u32[]{:S(2)}) async-start(bf16[5,3,16,24,384]{4,3,1,0,2:T(8,128)(2,1)} %copy.67), calls=%async_computation | async-start | bytes 8847360 | tf_op jit(solution)/shard_map/all_to_all | solution.py:603
  15.8 166.9 %gather_weights.1 = (bf16[2,384,3072]{2,1,0:T(8,128)(2,1)S(1)}, bf16[2,384,3072]{2,1,0:T(8,128)(2,1)S(1)}, bf16[8,384,768]{2,1,0:T(8,128)(2,1)}, f32[16,8,128]{2,1,0:T(8,128)S(1)}) custom-call(f32[48,24,384]{2,1,0:T(8,128)S(1)} %copy-done, f32[8,128]{1,0:T(8,128)S(1)} %pad_bitcast_fusion.1.vec_ref), custom_call_target="tpu_custom_call" | custom-call | tf_op jit(solution)/shard_map/gather_weights/pallas_call | solution.py:372
  187.2 4.1 convolution_bitcast_fusion
  192.4 6.0 %fusion.60 = (f32[12,512]{1,0:T(8,128)S(1)}, f32[12,512,512]{1,2,0:T(8,128)}) fusion(bf16[512,12,64]{0,2,1:T(8,128)(2,1)S(1)} %bitcast.139, bf16[512,12,64]{0,2,1:T(8,128)(2,1)S(1)} %bitcast.133, pred[512]{0:T(512)(128)(4,1)S(1)} %get-tuple-element.142), kind=kOutput, calls=%fused_computation.146 | convolution fusion | flops 412084224 | bytes 14180864 | tf_op jit(solution)/shard_map/while/body/eval_jaxpr/qhd,khd->hqk/dot_general | solution.py:54
  198.4 6.5 %fusion = f32[12,512]{1,0:T(8,128)S(1)} fusion(f32[12,512,512]{1,2,0:T(8,128)} %get-tuple-element.127, f32[12,512]{1,0:T(8,128)S(1)} %get-tuple-element.126), kind=kLoop, calls=%fused_computation.6 | loop fusion | flops 6285312 | bytes 12632064 | tf_op jit(solution)/shard_map/while/body/eval_jaxpr/reduce_sum | solution.py:70
  205.0 7.0 %fusion.35 = bf16[12,64,512]{2,1,0:T(8,128)(2,1)S(1)} fusion(bf16[512,12,64]{0,2,1:T(8,128)(2,1)S(1)} %bitcast.153, f32[12,512,512]{1,2,0:T(8,128)} %get-tuple-element.127, f32[12,512]{1,0:T(8,128)S(1)} %fusion, f32[12,512]{1,0:T(8,128)S(1)} %get-tuple-element.126), kind=kOutput, calls=%fused_computation.88 | convolution fusion | flops 412483584 | bytes 14204928 | tf_op jit(solution)/shard_map/while/body/eval_jaxpr/hqk,khd->qhd/dot_general | solution.py:72
  213.3 18.5 %multiply_convert_fusion.1 = (bf16[512,3072]{1,0:T(8,128)(2,1)S(1)}, f32[512,3072]{1,0:T(8,128)}, f32[512,3072]{1,0:T(8,128)}) fusion(f32[3072]{0:T(1024)S(1)} %add.169, bf16[768,3072]{1,0:T(8,128)(2,1)S(1)} %bitcast.128, f32[512,768]{1,0:T(8,128)S(1)} %get-tuple-element.129, f32[768]{0:T(1024)S(1)} %get-tuple-element.92, f32[768]{0:T(1024)S(1)} %get-tuple-element.93, ...), kind=kOutput, calls=%fused_computation.13 | convolution fusion | flops 2521694208 | bytes 22042624 | tf_op jit(solution)/shard_map/dot_general | solution.py:629
  231.9 2.8 fusion.62
  237.5 10.4 %fusion.63 = (f32[3072]{0:T(1024)S(1)}, bf16[512,3072]{1,0:T(8,128)(2,1)}) fusion(f32[512,3072]{1,0:T(8,128)} %get-tuple-element.107, bf16[3072,768]{1,0:T(8,128)(2,1)} %bitcast.163, f32[512,768]{1,0:T(8,128)S(1)} %get-tuple-element.105, f32[512]{0:T(512)S(1)} %negate_multiply_fusion.2, f32[512,3072]{1,0:T(8,128)} %get-tuple-element.130, f32[3072]{0:T(1024)S(1)} %add.169), kind=kOutput, calls=%fused_computation.149 | convolution fusion | flops 2441868288 | bytes 22046720 | tf_op jit(solution)/shard_map/td,fd->tf/dot_general | solution.py:644
  247.9 5.6 multiply_reduce_fusion.1
  258.6 10.6 %multiply_reduce_fusion = (f32[12,512]{1,0:T(8,128)S(1)}, f32[12,512,512]{1,2,0:T(8,128)}) fusion(f32[12,512,512]{1,2,0:T(8,128)} %get-tuple-element.127, f32[12,512]{1,0:T(8,128)S(1)} %log_add_fusion, bf16[512,12,64]{0,2,1:T(8,128)(2,1)S(1)} %bitcast.135, bf16[512,12,64]{0,2,1:T(8,128)(2,1)} %bitcast.154), kind=kOutput, calls=%fused_computation.1 | convolution fusion | flops 412084224 | bytes 26787840 | tf_op jit(solution)/shard_map/while/body/eval_jaxpr/qhd,khd->hqk/dot_general | solution.py:94
  271.4 6.8 %multiply_convert_fusion = bf16[12,512,512]{1,2,0:T(8,128)(2,1)S(1)} fusion(f32[12,512,512]{1,2,0:T(8,128)} %get-tuple-element.135, f32[12,512,512]{1,2,0:T(8,128)S(1)} %bitcast.131, f32[12,512]{1,0:T(8,128)S(1)} %get-tuple-element.134, f32[12,512]{1,0:T(8,128)S(1)} %log_add_fusion), kind=kLoop, calls=%fused_computation | loop fusion | flops 12582912 | bytes 31506432 | tf_op jit(solution)/shard_map/while/body/eval_jaxpr/convert_element_type | solution.py:100
  278.2 2.4 convert_reduce_fusion.1
  281.2 7.5 %convert_reduce_fusion = (f32[12,64]{1,0:T(8,128)S(1)}, bf16[12,64,512]{2,1,0:T(8,128)(2,1)}) fusion(bf16[512,12,64]{0,2,1:T(8,128)(2,1)S(1)} %bitcast.136, f32[12,512,512]{1,2,0:T(8,128)} %get-tuple-element.127, f32[12,512]{1,0:T(8,128)S(1)} %log_add_fusion), kind=kOutput, calls=%fused_computation.66 | convolution fusion | flops 410123520 | bytes 14183424 | tf_op jit(solution)/shard_map/while/body/eval_jaxpr/hqk,qhd->khd/dot_general | solution.py:91
  294.5 2.5 convolution_convert_fusion.3
  297.1 4.9 multiply_convert_fusion.2
  304.7 4.4 convolution_convert_fusion
  309.1 4.9 convolution_convert_fusion.1
  314.0 88.4 %reduce_gradients.1 = (bf16[3,384,384]{2,1,0:T(8,128)(2,1)S(1)}, f32[8,128]{1,0:T(8,128)S(1)}) custom-call(bf16[2,384,2304]{2,1,0:T(8,128)(2,1)S(1)} %bitcast.111, bf16[2,384,768]{2,1,0:T(8,128)(2,1)S(1)} %bitcast.112, bf16[2,384,3072]{2,1,0:T(8,128)(2,1)} %bitcast.142, bf16[8,384,768]{2,1,0:T(8,128)(2,1)} %bitcast.141, f32[16,8,128]{2,1,0:T(8,128)S(1)} %bitcast.117), custom_call_target="tpu_custom_call" | custom-call | tf_op jit(solution)/shard_map/reduce_gradients/pallas_call | solution.py:512
  402.5 2.7 fusion.59
  408.7 32.7 %soap_blocks.1 = (bf16[3,384,384]{2,1,0:T(8,128)(2,1)S(1)}, bf16[3,384,384]{2,1,0:T(8,128)(2,1)S(1)}, bf16[3,384,384]{2,1,0:T(8,128)(2,1)S(1)}, bf16[3,384,384]{2,1,0:T(8,128)(2,1)S(1)}) custom-call(bf16[3,384,384]{2,1,0:T(8,128)(2,1)S(1)} %get-tuple-element.78.grad, bf16[3,384,384]{2,1,0:T(8,128)(2,1)S(1)} %get-tuple-element.125.stat, ...), custom_call_target="tpu_custom_call" | custom-call | tf_op jit(solution)/shard_map/soap_blocks/pallas_call | solution.py:232
  442.1 4.5 copy.73
  446.6 5.3 all-to-all-start.1
  452.0 6.0 %add_bitcast_fusion = f32[1,512,768]{2,1,0:T(8,128)} fusion(bf16[768,3072]{1,0:T(8,128)(2,1)} %bitcast.121, f32[512,768]{1,0:T(8,128)S(1)} %copy-done.16, bf16[512,768]{0,1:T(8,128)(2,1)} %bitcast.158, bf16[512,768]{0,1:T(8,128)(2,1)} %bitcast.161, bf16[512,768]{0,1:T(8,128)(2,1)} %bitcast.155, f32[512]{0:T(512)S(1)} %negate_multiply_fusion.1), kind=kOutput, calls=%fused_computation.68 | convolution fusion | flops 1819803648 | bytes 9046016 | tf_op jit(solution)/shard_map/te,de->td/dot_general | solution.py:675
  458.0 72.1 %all-to-all-done.1 = bf16[4,3,1,384,384]{4,0,2,1,3:T(4,128)(2,1)} async-done(((bf16[4,3,1,384,384]{4,0,2,1,3:T(4,128)(2,1)}), bf16[4,3,1,384,384]{4,0,2,1,3:T(4,128)(2,1)}, u32[]{:S(2)}, u32[]{:S(2)}) %all-to-all-start.1) | async-done | bytes 3538976 | tf_op jit(solution)/shard_map/all_to_all | solution.py:712
  530.1 3.2 slice.156
  535.4 2.6 copy_convert_fusion
  538.0 2.9 copy-done.4
  544.1 2.3 fusion.15
  546.4 28.0 %collective-permute-done = bf16[2,48,24,384]{3,2,1,0:T(8,128)(2,1)S(1)} collective-permute-done((bf16[2,48,24,384]{3,2,1,0:T(8,128)(2,1)S(1)}, bf16[2,48,24,384]{3,2,1,0:T(8,128)(2,1)S(1)}, u32[]{:S(2)}, u32[]{:S(2)}) %collective-permute-start) | collective-permute-done | bytes 1769504 | tf_op jit(solution)/shard_map/ppermute | solution.py:719
  (168 shorter events, 43.6 us)
Async XLA Ops:
  8.6 7.2 %copy-start.25 = (f32[576]{0:T(1024)S(1)}, f32[576]{0:T(1024)}, u32[]{:S(2)}) copy-start(f32[576]{0:T(1024)} %param.23) | copy-start | bytes 6916
  8.6 7.2 %copy-start = (f32[48,24,384]{2,1,0:T(8,128)S(1)}, f32[48,24,384]{2,1,0:T(8,128)}, u32[]{:S(2)}) copy-start(f32[48,24,384]{2,1,0:T(8,128)} %mat_ref.1) | copy-start | bytes 5308420
  8.6 178.7 %copy-start.31 = (bf16[1,512,768]{2,1,0:T(8,128)(2,1)S(1)}, bf16[1,512,768]{2,1,0:T(8,128)(2,1)}, u32[]{:S(2)}) copy-start(bf16[1,512,768]{2,1,0:T(8,128)(2,1)} %param.13) | copy-start | bytes 2359300
  8.6 393.9 %all-to-all-start = ((bf16[5,3,16,24,384]{4,3,1,0,2:T(8,128)(2,1)}), bf16[5,3,16,24,384]{4,3,1,0,2:T(8,128)(2,1)}, u32[]{:S(2)}, u32[]{:S(2)}) async-start(bf16[5,3,16,24,384]{4,3,1,0,2:T(8,128)(2,1)} %copy.67), calls=%async_computation | async-start | bytes 8847360 | tf_op jit(solution)/shard_map/all_to_all | solution.py:603
  187.2 44.6 %copy-start.27 = (f32[768]{0:T(1024)}, f32[768]{0:T(1024)S(1)}, u32[]{:S(2)}) copy-start(f32[768]{0:T(1024)S(1)} %get-tuple-element.92) | copy-start | bytes 9220
  192.4 6.0 %copy-start.9 = (bf16[512,768]{0,1:T(8,128)(2,1)}, bf16[512,768]{0,1:T(8,128)(2,1)S(1)}, u32[]{:S(2)}) copy-start(bf16[512,768]{0,1:T(8,128)(2,1)S(1)} %get-tuple-element.112) | copy-start | bytes 2359300
  192.4 12.5 %copy-start.21 = (bf16[512,768]{0,1:T(8,128)(2,1)}, bf16[512,768]{0,1:T(8,128)(2,1)S(1)}, u32[]{:S(2)}) copy-start(bf16[512,768]{0,1:T(8,128)(2,1)S(1)} %get-tuple-element.113) | copy-start | bytes 2359300
  198.4 13.6 %slice-start = ((s8[4718592]{0:T(1024)(128)(4,1)}), s8[4194304]{0:T(1024)(128)(4,1)S(1)}, s32[]{:S(2)}) async-start(s8[4718592]{0:T(1024)(128)(4,1)} %bitcast.122), calls=%async_computation.2 | async-start | bytes 8388608
  204.9 8.4 %slice-start.2 = ((s8[4718592]{0:T(1024)(128)(4,1)}), s8[4194304]{0:T(1024)(128)(4,1)S(1)}, s32[]{:S(2)}) async-start(s8[4718592]{0:T(1024)(128)(4,1)} %bitcast.126), calls=%async_computation.4 | async-start | bytes 8388608
  204.9 7.0 %slice-start.1 = ((s8[4718592]{0:T(1024)(128)(4,1)}), s8[524288]{0:T(1024)(128)(4,1)S(1)}, s32[]{:S(2)}) async-start(s8[4718592]{0:T(1024)(128)(4,1)} %bitcast.122), calls=%async_computation.3 | async-start | bytes 1048576
  204.9 8.3 %slice-start.3 = ((s8[4718592]{0:T(1024)(128)(4,1)}), s8[524288]{0:T(1024)(128)(4,1)S(1)}, s32[]{:S(2)}) async-start(s8[4718592]{0:T(1024)(128)(4,1)} %bitcast.126), calls=%async_computation.5 | async-start | bytes 1048576
  212.0 19.9 %copy-start.33 = (bf16[12,64,512]{2,1,0:T(8,128)(2,1)}, bf16[12,64,512]{2,1,0:T(8,128)(2,1)S(1)}, u32[]{:S(2)}) copy-start(bf16[12,64,512]{2,1,0:T(8,128)(2,1)S(1)} %fusion.35) | copy-start | bytes 2359300
  212.0 19.8 %slice-start.8 = ((s8[4718592]{0:T(1024)(128)(4,1)}), s8[4194304]{0:T(1024)(128)(4,1)S(1)}, s32[]{:S(2)}) async-start(s8[4718592]{0:T(1024)(128)(4,1)} %bitcast.164), calls=%async_computation.10 | async-start | bytes 8388608
  212.9 40.6 %copy-start.17 = (f32[512,768]{1,0:T(8,128)}, f32[512,768]{1,0:T(8,128)S(1)}, u32[]{:S(2)}) copy-start(f32[512,768]{1,0:T(8,128)S(1)} %get-tuple-element.129) | copy-start | bytes 4718596
  213.3 18.5 %slice-start.9 = ((s8[4718592]{0:T(1024)(128)(4,1)}), s8[524288]{0:T(1024)(128)(4,1)S(1)}, s32[]{:S(2)}) async-start(s8[4718592]{0:T(1024)(128)(4,1)} %bitcast.164), calls=%async_computation.11 | async-start | bytes 1048576
  237.5 10.4 %copy-start.19 = (f32[512,768]{1,0:T(8,128)}, f32[512,768]{1,0:T(8,128)S(1)}, u32[]{:S(2)}) copy-start(f32[512,768]{1,0:T(8,128)S(1)} %get-tuple-element.105) | copy-start | bytes 4718596
  258.5 10.7 %slice-start.4 = ((s8[12582912]{0:T(1024)(128)(4,1)}), s8[4194304]{0:T(1024)(128)(4,1)S(1)}, s32[]{:S(2)}) async-start(s8[12582912]{0:T(1024)(128)(4,1)} %bitcast.130), calls=%async_computation.6 | async-start | bytes 8388608
  258.6 11.6 %slice-start.5 = ((s8[12582912]{0:T(1024)(128)(4,1)}), s8[4194304]{0:T(1024)(128)(4,1)S(1)}, s32[]{:S(2)}) async-start(s8[12582912]{0:T(1024)(128)(4,1)} %bitcast.130), calls=%async_computation.7 | async-start | bytes 8388608
  258.6 12.8 %slice-start.6 = ((s8[12582912]{0:T(1024)(128)(4,1)}), s8[4194304]{0:T(1024)(128)(4,1)S(1)}, s32[]{:S(2)}) async-start(s8[12582912]{0:T(1024)(128)(4,1)} %bitcast.130), calls=%async_computation.8 | async-start | bytes 8388608
  288.7 4.8 copy-start.8
  290.4 6.6 %copy-start.10 = (bf16[512,768]{0,1:T(8,128)(2,1)S(1)}, bf16[512,768]{0,1:T(8,128)(2,1)}, u32[]{:S(2)}) copy-start(bf16[512,768]{0,1:T(8,128)(2,1)} %copy-done.9) | copy-start | bytes 2359300
  297.0 5.0 copy-start.22
  297.0 5.0 copy-start.23
  297.0 5.0 copy-start.32
  304.7 4.4 copy-start.34
  446.6 5.4 copy-start.16
  446.6 83.5 %all-to-all-start.1 = ((bf16[4,3,1,384,384]{4,0,2,1,3:T(4,128)(2,1)}), bf16[4,3,1,384,384]{4,0,2,1,3:T(4,128)(2,1)}, u32[]{:S(2)}, u32[]{:S(2)}) async-start(bf16[4,3,1,384,384]{4,0,2,1,3:T(4,128)(2,1)} %copy.73), calls=%async_computation.1 | async-start | bytes 7077888 | tf_op jit(solution)/shard_map/all_to_all | solution.py:712
  458.0 76.8 %copy-start.26 = (f32[576]{0:T(1024)S(1)}, f32[576]{0:T(1024)}, u32[]{:S(2)}) copy-start(f32[576]{0:T(1024)} %param.23) | copy-start | bytes 6916
  458.0 76.8 %copy-start.29 = (f32[576]{0:T(1024)S(1)}, f32[576]{0:T(1024)}, u32[]{:S(2)}) copy-start(f32[576]{0:T(1024)} %param.25) | copy-start | bytes 6916
  458.0 76.8 %copy-start.30 = (f32[576]{0:T(1024)S(1)}, f32[576]{0:T(1024)}, u32[]{:S(2)}) copy-start(f32[576]{0:T(1024)} %param.24) | copy-start | bytes 6916
  533.6 40.9 %collective-permute-start = (bf16[2,48,24,384]{3,2,1,0:T(8,128)(2,1)S(1)}, bf16[2,48,24,384]{3,2,1,0:T(8,128)(2,1)S(1)}, u32[]{:S(2)}, u32[]{:S(2)}) collective-permute-start(bf16[2,48,24,384]{3,2,1,0:T(8,128)(2,1)S(1)} %bitcast.157), channel_id=1, source_target_pairs={{0,1},{1,0},{2,3},{3,2},{4,5},{5,4},{6,7},{7,6},{8,9},{9,8},{10,11... | collective-permute-start | bytes 5308424 | tf_op jit(solution)/shard_map/ppermute | solution.py:719
  544.1 30.3 %slice-start.7 = ((f32[4,3,1,384,384]{4,3,1,2,0:T(8,128)}), f32[2,3,1,384,384]{4,3,1,2,0:T(8,128)S(1)}, s32[]{:S(2)}) async-start(f32[4,3,1,384,384]{4,3,1,2,0:T(8,128)} %copy-done.4), calls=%async_computation.9 | async-start | bytes 7077888 | tf_op jit(solution)/shard_map/slice | solution.py:724
  (18 other events, 46.7 us)
